TPU v7x, 32 devices: a whole 2x2x4 slice. The times are simulated.
32 devices in a mesh: client: 8 (over z, x), shard: 4 (over y, core).
Axes of the slice: x: 2, y: 2, z: 4, core: 2. Of those that a mesh axis runs over, the one named last changes fastest.
Arguments:
- delta: bfloat16 [8, 4096, 14336], P('client', 'shard'), may hold values from -750 to 750
- start_coeffs: bfloat16 [14336, 64], replicated, may hold values from -0.046875 to 0.046875
- noise_p: float32 [2, 4096, 64], P(None, 'shard'), may hold values from -6 to 6
- noise_q: float32 [2, 14336, 64], P(None, 'shard'), may hold values from -6 to 6
Outputs:
- basis: float32 [4096, 64], P('shard')
- coeffs: float32 [14336, 64], P('shard')
All inputs are finite; a program needn't handle non-finite values.
Results may differ from a plain program's by a relative error of at most 0.0033.
Values may be sent and summed in bfloat16 or wider, within the bound.
A program may use at most 128 MiB of HBM per device.

v0:
```python
import math

import jax
import jax.numpy as jnp
from jax import lax
from jax.sharding import PartitionSpec as P

D = 4096
ITERS = 2


EPS = 1e-06
CLIP_FRACTION = 0.5


def clip_factor(mine):
    local = jnp.sum(jnp.square(mine.astype(jnp.float32)))
    total = lax.psum(local, "shard")
    count = mine.shape[0] * lax.axis_size("shard") * mine.shape[1]
    return jnp.minimum(1.0, CLIP_FRACTION * math.sqrt(count) / jnp.sqrt(total + EPS))


def noisy_panel(local_panel, level, noise):
    return lax.psum(local_panel, "client") + level * noise


def orthonormal(panel):
    local_gram = jnp.dot(
        panel.T, panel, precision=lax.Precision.HIGHEST, preferred_element_type=jnp.float32
    )
    gram = lax.psum(local_gram, "shard")
    lower = jnp.linalg.cholesky(gram)
    return jax.scipy.linalg.solve_triangular(lower, panel.T, lower=True).T


def on_device(delta, start_coeffs, noise_p, noise_q):
    mine = delta[0]
    rank = start_coeffs.shape[1]
    factor = clip_factor(mine)
    start_level = jnp.sqrt(jnp.sum(jnp.square(start_coeffs.astype(jnp.float32))) / rank)
    panel = jnp.zeros((mine.shape[0], rank), jnp.float32)
    own = mine.shape[1] // lax.axis_size("shard")
    coeffs = jnp.zeros((own, rank), jnp.float32)
    for step in range(ITERS):
        if step == 0:
            level = start_level
            local_panel = factor * jnp.dot(mine, start_coeffs, preferred_element_type=jnp.float32)
        else:
            level = jnp.sqrt(lax.psum(jnp.sum(jnp.square(coeffs)), "shard") / rank)
            qb = coeffs.astype(jnp.bfloat16)
            local_panel = factor * jnp.dot(
                mine,
                lax.all_gather(qb, "shard", axis=0, tiled=True),
                preferred_element_type=jnp.float32,
            )
        panel = orthonormal(noisy_panel(local_panel, level, noise_p[step]))
        pb = panel.astype(jnp.bfloat16)
        shares = lax.psum_scatter(
            factor * jnp.dot(mine.T, pb, preferred_element_type=jnp.float32),
            "shard",
            scatter_dimension=0,
            tiled=True,
        )
        coeffs = lax.psum(shares, "client") + noise_q[step]
    return (math.sqrt(D) * panel, coeffs)


def solution(mesh):
    placed = (P("client", "shard", None), P(), P(None, "shard", None), P(None, "shard", None))
    return jax.shard_map(
        on_device,
        mesh=mesh,
        in_specs=placed,
        out_specs=(P("shard", None), P("shard", None)),
        check_vma=False,
    )
```

profile of v0, /device:TPU:0, one launch (start us, length us, event | category | flops | bytes accessed | tf_op | source)
XLA Modules:
  0.0 563.6 jit_solution(17303590605497239346)
XLA Ops:
  7.2 0.0 all-reduce.5.cloned.1.call-start
  7.2 17.6 %multiply_reduce_fusion = f32[]{:T(128)} fusion(bf16[1,1024,14336]{2,1,0:T(8,128)(2,1)} %param.7), kind=kLoop, calls=%fused_computation | loop fusion | flops 44040192 | bytes 29360132 | tf_op jit(solution)/shard_map/reduce_sum | solution.py:17
  24.8 9.0 %psum.56 = f32[]{:T(128)} all-reduce(f32[]{:T(128)} %multiply_reduce_fusion), channel_id=1, replica_groups=mesh['client'=8,'shard'=4] {'shard'}, use_global_device_ids=true, to_apply=%region_1.0 | all-reduce | flops 1 | bytes 8 | tf_op jit(solution)/shard_map/psum | solution.py:18
  34.5 15.1 %fusion.20 = f32[1024,64]{0,1:T(8,128)} fusion(bf16[14336,64]{0,1:T(8,128)(2,1)S(1)} %copy-done, bf16[1,1024,14336]{2,1,0:T(8,128)(2,1)} %param.7, f32[]{:T(128)S(6)} %min_shard_map.3), kind=kOutput, calls=%fused_computation.14 | convolution fusion | flops 1879113728 | bytes 31457284 | tf_op jit(solution)/shard_map/dot_general | solution.py:47
  49.6 0.0 all-reduce.5.cloned.1.call-update
  49.6 0.0 reduce-scatter.3.cloned.1.call-start
  49.7 1.5 multiply_reduce_fusion.1
  51.9 68.7 %all-reduce.5.cloned.1.call-done = f32[1024,64]{0,1:T(8,128)} async-done(((f32[1024,64]{0,1:T(8,128)}), f32[1024,64]{0,1:T(8,128)}) %all-reduce.5.cloned.1.call-update) | async-done | bytes 262160 | tf_op jit(solution)/shard_map/psum | solution.py:24
  120.6 1.4 fusion.34
  122.1 10.3 %psum.58 = f32[64,64]{0,1:T(8,128)S(1)} all-reduce(f32[64,64]{0,1:T(8,128)S(1)} %fusion.34), channel_id=1, replica_groups=mesh['client'=8,'shard'=4] {'shard'}, use_global_device_ids=true, to_apply=%region_4.0 | all-reduce | flops 4096 | bytes 32768 | tf_op jit(solution)/shard_map/psum | solution.py:31
  132.3 0.1 copy.7
  132.4 5.8 %cholesky.44 = f32[64,64]{1,0:T(8,128)S(1)} custom-call(f32[64,64]{1,0:T(8,128)S(1)} %fusion.41), custom_call_target="Cholesky" | custom-call | tf_op jit(solution)/shard_map/jit(cholesky)/cholesky | solution.py:32
  138.3 0.6 compare_reduce_fusion.1
  138.9 0.7 fusion.36
  139.6 4.9 custom-call.6
  144.5 1.4 convolution_convert_fusion
  145.9 16.4 %fusion.11 = f32[14336,64]{0,1:T(8,128)} fusion(bf16[64,1024]{1,0:T(8,128)(2,1)S(1)} %convolution_convert_fusion, bf16[1,1024,14336]{2,1,0:T(8,128)(2,1)} %param.7, f32[]{:T(128)S(6)} %min_shard_map.3), kind=kOutput, calls=%fused_computation.10 | convolution fusion | flops 1879965696 | bytes 33161220 | tf_op jit(solution)/shard_map/dot_general | solution.py:59
  162.2 0.0 reduce-scatter.3.cloned.1.call-update
  162.3 0.2 all-reduce.7.cloned.1.call-start
  162.5 40.6 %reduce-scatter.3.cloned.1.call-done = f32[3584,64]{0,1:T(8,128)} async-done(((f32[14336,64]{0,1:T(8,128)}), f32[3584,64]{0,1:T(8,128)}) %reduce-scatter.3.cloned.1.call-update) | async-done | bytes 917520 | tf_op jit(solution)/shard_map/reduce_scatter | solution.py:58
  203.1 0.0 all-reduce.7.cloned.1.call-update
  203.1 0.0 all-gather.2.cloned.1.call-start
  203.2 80.0 %all-reduce.7.cloned.1.call-done = f32[3584,64]{0,1:T(8,128)} async-done(((f32[3584,64]{0,1:T(8,128)}), f32[3584,64]{0,1:T(8,128)}) %all-reduce.7.cloned.1.call-update) | async-done | bytes 917520 | tf_op jit(solution)/shard_map/psum | solution.py:64
  283.2 2.7 multiply_reduce_fusion.2
  285.9 0.0 all-gather.2.cloned.1.call-update
  286.0 0.0 all-reduce.9.cloned.1.call-start
  286.0 20.0 %all-gather.2.cloned.1.call-done = bf16[14336,64]{0,1:T(8,128)(2,1)} async-done(((bf16[3584,64]{0,1:T(8,128)(2,1)}), bf16[14336,64]{0,1:T(8,128)(2,1)}) %all-gather.2.cloned.1.call-update) | async-done | bytes 1835024 | tf_op jit(solution)/shard_map/all_gather | solution.py:53
  306.1 15.5 %fusion.26 = f32[1024,64]{0,1:T(8,128)} fusion(bf16[14336,64]{0,1:T(8,128)(2,1)} %all-gather.2.cloned.1.call-done, bf16[1,1024,14336]{2,1,0:T(8,128)(2,1)} %param.7, f32[]{:T(128)S(6)} %min_shard_map.3), kind=kOutput, calls=%fused_computation.16 | convolution fusion | flops 1879113728 | bytes 31457284 | tf_op jit(solution)/shard_map/dot_general | solution.py:51
  321.5 0.0 all-reduce.9.cloned.1.call-update
  321.6 0.0 reduce-scatter.5.cloned.1.call-start
  321.6 6.4 %psum.61 = f32[]{:T(128)} all-reduce(f32[]{:T(128)} %get-tuple-element.4), channel_id=1, replica_groups=mesh['client'=8,'shard'=4] {'shard'}, use_global_device_ids=true, to_apply=%region_11.0 | all-reduce | flops 1 | bytes 8 | tf_op jit(solution)/shard_map/psum | solution.py:49
  328.7 63.6 %all-reduce.9.cloned.1.call-done = f32[1024,64]{0,1:T(8,128)} async-done(((f32[1024,64]{0,1:T(8,128)}), f32[1024,64]{0,1:T(8,128)}) %all-reduce.9.cloned.1.call-update) | async-done | bytes 262160 | tf_op jit(solution)/shard_map/psum | solution.py:24
  392.3 1.4 fusion.35
  393.7 10.3 %psum.62 = f32[64,64]{0,1:T(8,128)S(1)} all-reduce(f32[64,64]{0,1:T(8,128)S(1)} %fusion.35), channel_id=1, replica_groups=mesh['client'=8,'shard'=4] {'shard'}, use_global_device_ids=true, to_apply=%region_12.0 | all-reduce | flops 4096 | bytes 32768 | tf_op jit(solution)/shard_map/psum | solution.py:31
  403.9 0.1 copy.9
  404.0 5.8 %cholesky.55 = f32[64,64]{1,0:T(8,128)S(1)} custom-call(f32[64,64]{1,0:T(8,128)S(1)} %fusion.39), custom_call_target="Cholesky" | custom-call | tf_op jit(solution)/shard_map/jit(cholesky)/cholesky | solution.py:32
  409.9 0.6 compare_reduce_fusion
  410.6 0.7 fusion.37
  411.2 4.9 custom-call.7
  416.1 1.4 fusion.30
  417.5 16.3 %fusion.17 = f32[14336,64]{0,1:T(8,128)} fusion(bf16[1,1024,14336]{2,1,0:T(8,128)(2,1)} %param.7, f32[]{:T(128)S(6)} %min_shard_map.3, f32[64,1024]{1,0:T(8,128)S(1)} %fusion.30), kind=kOutput, calls=%fused_computation.12 | convolution fusion | flops 1880031232 | bytes 33292292 | tf_op jit(solution)/shard_map/dot_general | solution.py:59
  433.9 0.0 reduce-scatter.5.cloned.1.call-update
  433.9 0.0 all-reduce.11.cloned.1.call-start
  433.9 40.8 %reduce-scatter.5.cloned.1.call-done = f32[3584,64]{0,1:T(8,128)} async-done(((f32[14336,64]{0,1:T(8,128)}), f32[3584,64]{0,1:T(8,128)}) %reduce-scatter.5.cloned.1.call-update) | async-done | bytes 917520 | tf_op jit(solution)/shard_map/reduce_scatter | solution.py:58
  474.7 0.0 all-reduce.11.cloned.1.call-update
  474.8 0.7 multiply_bitcast_fusion
  475.5 79.1 %all-reduce.11.cloned.1.call-done = f32[3584,64]{0,1:T(8,128)} async-done(((f32[3584,64]{0,1:T(8,128)}), f32[3584,64]{0,1:T(8,128)}) %all-reduce.11.cloned.1.call-update) | async-done | bytes 917520 | tf_op jit(solution)/shard_map/psum | solution.py:64
  554.6 2.2 bitcast_add_fusion
  (12 shorter events, 0.1 us)
Async XLA Ops:
  7.2 27.3 %copy-start = (bf16[14336,64]{0,1:T(8,128)(2,1)S(1)}, bf16[14336,64]{0,1:T(8,128)(2,1)}, u32[]{:S(2)}) copy-start(bf16[14336,64]{0,1:T(8,128)(2,1)} %param.8) | copy-start | bytes 5505028
  7.2 113.5 %all-reduce.5.cloned.1.call-start = ((), (), s32[]{:S(2)}) async-start(), calls=%async_computation.2 | async-start | bytes 524288 | tf_op jit(solution)/shard_map/psum | solution.py:24
  34.5 86.2 %copy-start.1 = (f32[2,1024,64]{1,2,0:T(8,128)S(1)}, f32[2,1024,64]{1,2,0:T(8,128)}, u32[]{:S(2)}) copy-start(f32[2,1024,64]{1,2,0:T(8,128)} %param.9) | copy-start | bytes 1572868
  49.6 153.5 %reduce-scatter.3.cloned.1.call-start = ((), (), s32[]{:S(2)}) async-start(), calls=%async_computation.3 | async-start | bytes 4587520 | tf_op jit(solution)/shard_map/reduce_scatter | solution.py:58
  162.2 121.0 %copy-start.2 = (f32[2,3584,64]{1,2,0:T(8,128)S(1)}, f32[2,3584,64]{1,2,0:T(8,128)}, u32[]{:S(2)}) copy-start(f32[2,3584,64]{1,2,0:T(8,128)} %param.10) | copy-start | bytes 5505028
  162.3 120.9 %all-reduce.7.cloned.1.call-start = ((), (), s32[]{:S(2)}) async-start(), calls=%async_computation.4 | async-start | bytes 1835008 | tf_op jit(solution)/shard_map/psum | solution.py:64
  203.1 102.9 %all-gather.2.cloned.1.call-start = ((), (), s32[]{:S(2)}) async-start(), calls=%async_computation.5 | async-start | bytes 2293760 | tf_op jit(solution)/shard_map/all_gather | solution.py:53
  286.0 106.3 %all-reduce.9.cloned.1.call-start = ((), (), s32[]{:S(2)}) async-start(), calls=%async_computation.6 | async-start | bytes 524288 | tf_op jit(solution)/shard_map/psum | solution.py:24
  321.6 153.2 %reduce-scatter.5.cloned.1.call-start = ((), (), s32[]{:S(2)}) async-start(), calls=%async_computation.7 | async-start | bytes 4587520 | tf_op jit(solution)/shard_map/reduce_scatter | solution.py:58
  433.9 120.7 %copy-start.3 = (f32[2,3584,64]{1,2,0:T(8,128)S(1)}, f32[2,3584,64]{1,2,0:T(8,128)}, u32[]{:S(2)}) copy-start(f32[2,3584,64]{1,2,0:T(8,128)} %param.10) | copy-start | bytes 5505028
  433.9 120.7 %all-reduce.11.cloned.1.call-start = ((), (), s32[]{:S(2)}) async-start(), calls=%async_computation.8 | async-start | bytes 1835008 | tf_op jit(solution)/shard_map/psum | solution.py:64
Sparse Core Ops, SparseCore 0:
  49.8 70.8 all-reduce.4
  162.4 40.6 reduce-scatter.2
  206.6 76.5 all-reduce.6
  286.1 19.9 all-gather.1
  321.7 70.5 all-reduce.8
  434.0 40.6 reduce-scatter.4
  478.2 76.3 all-reduce.10
where the time goes:
time: 564 us
  waiting for transfers between devices  393 us (70%)
  matrix products  68.9 us (12%)
  other arithmetic  48.9 us (9%)
  blocking collectives  35.9 us (6%)
  between operations  16.3 us (3%)
    psum x2, waiting for transfers between devices, on_device(): coeffs = lax.psum(shares, 'client') + noise_q[step]  159 us
    psum x2, waiting for transfers between devices, noisy_panel(): return lax.psum(local_panel, 'client') + level * noise  132 us
    reduce_scatter x2, waiting for transfers between devices, on_device(): lax.psum_scatter(factor * jnp.dot(mine.T, pb, preferred_element_type=jnp....  81.4 us
    dot_general x2, matrix products, on_device(): jnp.dot(mine.T, pb, preferred_element_type=jnp.float32)  32.7 us
    psum x2, blocking collectives, orthonormal(): gram = lax.psum(local_gram, 'shard')  20.5 us
    all_gather x1, waiting for transfers between devices, on_device(): lax.all_gather(qb, 'shard', axis=0, tiled=True)  20 us
    reduce_sum x1, other arithmetic, clip_factor(): local = jnp.sum(jnp.square(mine.astype(jnp.float32)))  17.6 us
    dot_general x1, matrix products, on_device(): jnp.dot(mine, lax.all_gather(qb, 'shard', axis=0, tiled=True), preferred_...  15.5 us
  transfers between devices with their start and end apart: 7, of which 7 were waited for; matrix products, arithmetic and copies ran while one was open for 0% of the time, Pallas kernels for 0%

commit v1 on v0

v1 whole, which is shorter than its diff:
```python
import functools
import math

import jax
import jax.numpy as jnp
from jax import lax
from jax.experimental import pallas as pl
from jax.experimental.pallas import tpu as pltpu
from jax.sharding import PartitionSpec as P

ITERS = 2
EPS = 1e-06
CLIP_FRACTION = 0.5
LANES = 128
MESH = pl.DeviceIdType.MESH
F32 = jnp.float32
BF16 = jnp.bfloat16
HIGH = lax.Precision.HIGHEST


def nt(a, b, precision=None):
    return lax.dot_general(
        a, b, (((1,), (1,)), ((), ())), precision=precision, preferred_element_type=F32
    )


def inverse_lower(gram):
    n = gram.shape[0]
    rows = lax.broadcasted_iota(jnp.int32, (n, n), 0)
    cols = lax.broadcasted_iota(jnp.int32, (n, n), 1)
    work = jnp.concatenate([gram, (rows == cols).astype(F32)], axis=1)
    at = lax.broadcasted_iota(jnp.int32, (n, 2 * n), 0)
    out = jnp.zeros((n, 2 * n), F32)
    for j in range(n):
        row = work[j : j + 1, :]
        root = 1.0 / jnp.sqrt(row[:, j : j + 1])
        row = row * root
        out = jnp.where(at == j, row, out)
        if j < n - 1:
            work = work - (work[:, j : j + 1] * root) * row
    return out[:, n:]


def kernel(
    sizes, delta_hbm, start, noise_p, noise_q, basis_ref, coeffs_ref,
    delta, acc, sq_buf, sq_all, p_send, p_recv, p_own, p_all, g_buf, pb,
    core_send, core_recv, own, y_send, y_recv, z_send, z_recv, q_own, q_piece, q_all,
    l_own, l_client, l_part, l_shard,
    load_sem, small_send, small_recv, p_sems, g_sems, core_sems, y_sems, z_sems,
    a_sems, ay_sems, ac_sems, lc_sems, ls_sems,
):
    clients, shards, sub, units, unit, chunks = sizes
    ys = shards // 2
    rows, full = delta.shape
    rank = start.shape[1]
    piece = rows // clients
    wide = sub * LANES
    span = units * wide
    me_c = lax.axis_index("client")
    me_s = lax.axis_index("shard")
    core = lax.rem(me_s, 2)
    me_y = me_s // 2

    chunk = full // chunks

    def load(i):
        return pltpu.make_async_copy(
            delta_hbm.at[0, :, pl.ds(i * chunk, chunk)],
            delta.at[:, pl.ds(i * chunk, chunk)],
            load_sem.at[i],
        )

    for i in range(chunks):
        load(i).start()

    barrier = pltpu.get_barrier_semaphore()
    for d in range(1, clients):
        pl.semaphore_signal(
            barrier, inc=1, device_id=(lax.rem(me_c + d, clients), me_s), device_id_type=MESH
        )
    for d in range(1, shards):
        pl.semaphore_signal(
            barrier, inc=1, device_id=(me_c, lax.rem(me_s + d, shards)), device_id_type=MESH
        )

    def send(src, dst, sems, index, device):
        return pltpu.make_async_remote_copy(
            src_ref=src, dst_ref=dst,
            send_sem=sems.at[(0,) + index], recv_sem=sems.at[(1,) + index],
            device_id=device, device_id_type=MESH,
        )

    def to_client(d):
        return (lax.rem(me_c + d, clients), me_s)

    def to_shard(d):
        return (me_c, lax.rem(me_s + d, shards))

    def start_sum(i, total):
        v = start[pl.ds(pl.multiple_of(i * wide, wide), wide), :].astype(F32)
        return total + jnp.sum(v * v, axis=0, keepdims=True)

    level0 = jnp.sqrt(
        jnp.sum(lax.fori_loop(0, full // wide, start_sum, jnp.zeros((1, rank), F32)), axis=1, keepdims=True)
        / rank
    )

    acc[...] = jnp.zeros_like(acc)
    step = 512
    total = jnp.zeros((8, step), F32)
    for i in range(chunks):
        load(i).wait()

        def first(j, total, i=i):
            at = pl.multiple_of(i * chunk + j * step, step)
            acc[...] += jnp.dot(
                delta[:, pl.ds(at, step)], start[pl.ds(at, step), :], preferred_element_type=F32
            )

            def squares(r, t):
                v = delta[pl.ds(pl.multiple_of(r * 128, 128), 128), pl.ds(at, step)].astype(F32)
                return t + jnp.sum((v * v).reshape(16, 8, step), axis=0)

            return lax.fori_loop(0, rows // 128, squares, total)

        total = lax.fori_loop(0, chunk // step, first, total)

    pl.semaphore_wait(barrier, clients + shards - 2)

    mine = jnp.sum(jnp.sum(total, axis=0, keepdims=True), axis=1, keepdims=True)
    sq_buf[...] = jnp.broadcast_to(mine, (8, LANES))
    for d in range(1, shards):
        pltpu.make_async_remote_copy(
            src_ref=sq_buf, dst_ref=sq_all.at[d - 1],
            send_sem=small_send.at[d - 1], recv_sem=small_recv.at[d - 1],
            device_id=to_shard(d), device_id_type=MESH,
        ).start()
    sumsq = sq_buf[0:1, 0:1]
    for d in range(1, shards):
        c = pltpu.make_async_remote_copy(
            src_ref=sq_buf, dst_ref=sq_all.at[d - 1],
            send_sem=small_send.at[d - 1], recv_sem=small_recv.at[d - 1],
            device_id=to_shard(d), device_id_type=MESH,
        )
        c.wait()
        sumsq = sumsq + sq_all[d - 1, 0:1, 0:1]
    count = rows * shards * full
    factor = jnp.minimum(1.0, CLIP_FRACTION * math.sqrt(count) / jnp.sqrt(sumsq + EPS))

    for it in range(ITERS):
        if it == 0:
            level = level0
        else:
            acc[...] = jnp.zeros_like(acc)

            def again(n, _):
                b = n // units
                k = lax.rem(n, units)
                at = pl.multiple_of(b * span + k * wide, LANES)
                v = q_all[b, k].astype(F32).reshape(sub * rank, LANES)
                v = jnp.concatenate([v[t * rank : (t + 1) * rank] for t in range(sub)], axis=1)
                acc[...] += nt(delta[:, pl.ds(at, wide)], v.astype(BF16))
                return 0

            lax.fori_loop(0, shards * units, again, 0)

        for d in range(clients):
            c = lax.rem(me_c + d, clients)
            v = acc[pl.ds(pl.multiple_of(c * piece, piece), piece), :] * factor
            p_send[it, d] = v.T
        copies = [
            send(p_send.at[it, d], p_recv.at[it, d], p_sems, (it, 0, d), to_client(d))
            for d in range(1, clients)
        ]
        for c in copies:
            c.start()
        v = p_send[it, 0] + level * noise_p[it]
        for d, c in enumerate(copies, 1):
            c.wait()
            v = v + p_recv[it, d]
        p_own[it] = v
        copies = [
            send(p_own.at[it], p_all.at[it, me_c], p_sems, (it, 1, d), to_client(d))
            for d in range(1, clients)
        ]
        for c in copies:
            c.start()
        p_all[it, me_c] = v
        for c in copies:
            c.wait()

        gram = jnp.zeros((rank, rank), F32)
        for c in range(clients):
            v = p_all[it, c]
            gram = gram + nt(v, v, HIGH)
        g_buf[it, 0] = gram
        copies = [
            send(g_buf.at[it, 0], g_buf.at[it, d], g_sems, (it, d), to_shard(d))
            for d in range(1, shards)
        ]
        for c in copies:
            c.start()
        for d, c in enumerate(copies, 1):
            c.wait()
            gram = gram + g_buf[it, d]
        inverse = inverse_lower(gram)
        for c in range(clients):
            v = jnp.dot(inverse, p_all[it, c], precision=HIGH, preferred_element_type=F32)
            pb[:, c * piece : (c + 1) * piece] = v.astype(BF16)
            if it == ITERS - 1:
                basis_ref[c] = v * math.sqrt(rows * shards)

        def block(owner, k):
            at = pl.multiple_of(owner * span + k * wide, LANES)
            v = factor * jnp.dot(pb[...], delta[:, pl.ds(at, wide)], preferred_element_type=F32)
            v = jnp.concatenate([v[:, t * LANES : (t + 1) * LANES] for t in range(sub)], axis=0)
            return v.reshape(clients, unit, LANES)

        sends = []
        y_copies = []
        for dy in list(range(1, ys)) + [0]:
            to_y = lax.rem(me_y + dy, ys)

            def other(k, _, to_y=to_y, dy=dy):
                core_send[it, dy, k] = block(2 * to_y + 1 - core, k)
                return 0

            lax.fori_loop(0, units, other, 0)
            c = send(core_send.at[it, dy], core_recv.at[it, dy], core_sems, (it, dy), (me_c, 2 * me_y + 1 - core))
            c.start()

            def same(k, _, to_y=to_y):
                own[k] = block(2 * to_y + core, k)
                return 0

            lax.fori_loop(0, units, same, 0)
            c.wait()
            if dy > 0:

                def add(k, _, dy=dy):
                    y_send[it, dy - 1, k] = (own[k] + core_recv[it, dy, k]).astype(BF16)
                    return 0

                lax.fori_loop(0, units, add, 0)
                c = send(y_send.at[it, dy - 1], y_recv.at[it, dy - 1], y_sems, (it, dy - 1), (me_c, 2 * to_y + core))
                c.start()
                y_copies.append(c)
        for c in y_copies:
            c.wait()

        def add_z(k, _):
            v = own[k] + core_recv[it, 0, k]
            for d in range(1, ys):
                v = v + y_recv[it, d - 1, k].astype(F32)
            own[k] = v
            for c in range(clients):
                z_send[it, c, k] = v[c].astype(BF16)
            return 0

        lax.fori_loop(0, units, add_z, 0)
        copies = [
            send(z_send.at[it, lax.rem(me_c + d, clients)], z_recv.at[it, d], z_sems, (it, d), to_client(d))
            for d in range(1, clients)
        ]
        for c in copies:
            c.start()
        for c in copies:
            c.wait()

        if it < ITERS - 1:
            square = jnp.zeros((1, LANES), F32)
            for k in range(units):
                v = own[k, me_c] + noise_q[k]
                for d in range(1, clients):
                    v = v + z_recv[it, d, k].astype(F32)
                q_piece[k] = v.astype(BF16)
                square = square + jnp.sum(v * v, axis=0, keepdims=True)
            part = jnp.sum(square, axis=1, keepdims=True)
            l_own[...] = jnp.broadcast_to(part, (8, LANES))
            q_all[me_s, :, me_c] = q_piece[...]
            copies = [
                send(q_piece, q_all.at[me_s, :, me_c], a_sems, (d,), to_client(d))
                for d in range(1, clients)
            ]
            l_copies = [send(l_own, l_client.at[d - 1], lc_sems, (d,), to_client(d)) for d in range(1, clients)]
            for c in copies + l_copies:
                c.start()
            later = []

            def pass_on(d):
                who = lax.rem(me_c + clients - d, clients)
                here = q_all.at[me_s, :, who]
                for dy in range(1, ys):
                    c = send(here, here, ay_sems, (d, dy - 1), (me_c, 2 * lax.rem(me_y + dy, ys) + core))
                    c.start()
                    later.append(c)
                c = send(here, here, ac_sems, (d, 0), (me_c, 2 * me_y + 1 - core))
                c.start()
                later.append(c)

            pass_on(0)
            for d, c in enumerate(copies, 1):
                c.wait_recv()
                pass_on(d)
            for d, c in enumerate(l_copies, 1):
                c.wait()
                part = part + l_client[d - 1, 0:1, 0:1]
            l_part[...] = jnp.broadcast_to(part, (8, LANES))
            l_copies = [send(l_part, l_shard.at[d - 1], ls_sems, (d,), to_shard(d)) for d in range(1, shards)]
            for c in l_copies:
                c.start()
            for d in range(clients):
                who = lax.rem(me_c + clients - d, clients)
                for dy in range(1, ys):
                    from_s = 2 * lax.rem(me_y + ys - dy, ys) + core
                    here = q_all.at[from_s, :, who]
                    send(here, here, ay_sems, (d, dy - 1), (me_c, me_s)).wait_recv()
                    c = send(here, here, ac_sems, (d, dy), (me_c, 2 * me_y + 1 - core))
                    c.start()
                    sends.append(c)
            for d in range(clients):
                who = lax.rem(me_c + clients - d, clients)
                for dy in range(ys):
                    from_s = 2 * lax.rem(me_y + ys - dy, ys) + 1 - core
                    here = q_all.at[from_s, :, who]
                    send(here, here, ac_sems, (d, dy), (me_c, me_s)).wait_recv()
            for c in later + sends + copies:
                c.wait_send()
            for d, c in enumerate(l_copies, 1):
                c.wait()
                part = part + l_shard[d - 1, 0:1, 0:1]
            level = jnp.sqrt(part / rank)
        else:
            for k in range(units):
                v = own[k, me_c]
                for d in range(1, clients):
                    v = v + z_recv[it, d, k].astype(F32)
                q_own[k] = v
            coeffs_ref[:, me_c] = q_own[...]
            copies = [
                send(q_own, coeffs_ref.at[:, me_c], a_sems, (clients + d,), to_client(d))
                for d in range(1, clients)
            ]
            for c in copies:
                c.start()
            for c in copies:
                c.wait()


def on_device(clients, shards, delta, start_coeffs, noise_p, noise_q):
    rows, full = delta.shape[1:]
    rank = start_coeffs.shape[1]
    ys = shards // 2
    piece = rows // clients
    tiles = full // shards // LANES
    sub = next(
        s for s in range(1, tiles + 1)
        if tiles % s == 0 and (s * rank) % (8 * clients) == 0 and s * rank >= 32 * clients
    )
    units = tiles // sub
    unit = sub * rank // clients
    chunks = 7
    me = lax.axis_index("client")

    own_p = lax.dynamic_slice_in_dim(noise_p, me * piece, piece, axis=1).transpose(0, 2, 1)
    slabs = noise_q.reshape(ITERS, units, sub, LANES, rank).transpose(0, 1, 2, 4, 3)
    slabs = slabs.reshape(ITERS, units, clients, unit, LANES)
    own_q = lax.dynamic_index_in_dim(slabs[0], me, axis=1, keepdims=False)

    dma = pltpu.SemaphoreType.DMA
    basis, coeffs = pl.pallas_call(
        functools.partial(kernel, (clients, shards, sub, units, unit, chunks)),
        out_shape=(
            jax.ShapeDtypeStruct((clients, rank, piece), F32),
            jax.ShapeDtypeStruct((units, clients, unit, LANES), F32),
        ),
        in_specs=[pl.BlockSpec(memory_space=pl.ANY)] + [pl.BlockSpec(memory_space=pltpu.VMEM)] * 3,
        out_specs=[pl.BlockSpec(memory_space=pltpu.VMEM)] * 2,
        scratch_shapes=[
            pltpu.VMEM((rows, full), BF16),
            pltpu.VMEM((rows, rank), F32),
            pltpu.VMEM((8, LANES), F32),
            pltpu.VMEM((shards - 1, 8, LANES), F32),
            pltpu.VMEM((ITERS, clients, rank, piece), F32),
            pltpu.VMEM((ITERS, clients, rank, piece), F32),
            pltpu.VMEM((ITERS, rank, piece), F32),
            pltpu.VMEM((ITERS, clients, rank, piece), F32),
            pltpu.VMEM((ITERS, shards, rank, rank), F32),
            pltpu.VMEM((rank, rows), BF16),
            pltpu.VMEM((ITERS, ys, units, clients, unit, LANES), F32),
            pltpu.VMEM((ITERS, ys, units, clients, unit, LANES), F32),
            pltpu.VMEM((units, clients, unit, LANES), F32),
            pltpu.VMEM((ITERS, ys - 1, units, clients, unit, LANES), BF16),
            pltpu.VMEM((ITERS, ys - 1, units, clients, unit, LANES), BF16),
            pltpu.VMEM((ITERS, clients, units, unit, LANES), BF16),
            pltpu.VMEM((ITERS, clients, units, unit, LANES), BF16),
            pltpu.VMEM((units, unit, LANES), F32),
            pltpu.VMEM((units, unit, LANES), BF16),
            pltpu.VMEM((shards, units, clients, unit, LANES), BF16),
            pltpu.VMEM((8, LANES), F32),
            pltpu.VMEM((clients - 1, 8, LANES), F32),
            pltpu.VMEM((8, LANES), F32),
            pltpu.VMEM((shards - 1, 8, LANES), F32),
            dma((chunks,)),
            dma((shards - 1,)),
            dma((shards - 1,)),
            dma((2, ITERS, 2, clients)),
            dma((2, ITERS, shards)),
            dma((2, ITERS, ys)),
            dma((2, ITERS, ys)),
            dma((2, ITERS, clients)),
            dma((2, 2 * clients)),
            dma((2, clients, ys)),
            dma((2, clients, ys)),
            dma((2, clients)),
            dma((2, shards)),
        ],
        compiler_params=pltpu.CompilerParams(
            collective_id=0, has_side_effects=True, vmem_limit_bytes=60 * 1024 * 1024
        ),
        cost_estimate=pl.CostEstimate(
            flops=8 * rows * full * rank, bytes_accessed=2 * rows * full, transcendentals=0
        ),
    )(delta, start_coeffs, own_p, own_q)
    basis = basis.transpose(0, 2, 1).reshape(rows, rank)
    coeffs = coeffs.reshape(units, sub, rank, LANES).transpose(0, 1, 3, 2).reshape(full // shards, rank)
    return basis, coeffs + noise_q[ITERS - 1]


def solution(mesh):
    placed = (P("client", "shard", None), P(), P(None, "shard", None), P(None, "shard", None))
    return jax.shard_map(
        functools.partial(on_device, mesh.shape["client"], mesh.shape["shard"]),
        mesh=mesh,
        in_specs=placed,
        out_specs=(P("shard", None), P("shard", None)),
        check_vma=False,
    )
```

time: 564 us -> 200 us (0.35)
  waiting for transfers between devices: 393 us -> 0 us
  Pallas kernels: 0 us -> 181 us
  matrix products: 68.9 us -> 0 us
  other arithmetic: 48.9 us -> 2.2 us
  blocking collectives: 35.9 us -> 0 us
  between operations: 16.3 us -> 0.69 us
  local copies, waits for them, and re-layouts: 0.17 us -> 13 us
    psum x4 -> x0, waiting for transfers between devices: 291 us -> none  [the longest x2 159 us: on_device(): coeffs = lax.psum(shares, 'client') + noise_q[step]]
    pallas_call x0 -> x1, Pallas kernels: none -> 181 us  [on_device(): pl.pallas_call(functools.partial(kernel, (clients, shards, sub, units, un...]
    reduce_scatter x2 -> x0, waiting for transfers between devices: 81.4 us -> none  [on_device(): lax.psum_scatter(factor * jnp.dot(mine.T, pb, preferred_element_type=jnp....]
    dot_general x6 -> x0, matrix products: 66.1 us -> none  [the longest x2 32.7 us: on_device(): jnp.dot(mine.T, pb, preferred_element_type=jnp.float32)]
    psum x4 -> x0, blocking collectives: 35.9 us -> none  [the longest x2 20.5 us: orthonormal(): gram = lax.psum(local_gram, 'shard')]
    another operation x10 -> x0, other arithmetic: 24.1 us -> none  [the longest x6 13 us: orthonormal(): lower = jnp.linalg.cholesky(gram)]
    reduce_sum x3 -> x0, other arithmetic: 21.8 us -> none  [the longest x1 17.6 us: clip_factor(): local = jnp.sum(jnp.square(mine.astype(jnp.float32)))]
    all_gather x1 -> x0, waiting for transfers between devices: 20 us -> none  [on_device(): lax.all_gather(qb, 'shard', axis=0, tiled=True)]
  transfers between devices with their start and end apart: 7 -> 0, of which waited for: 7 -> 0; matrix products, arithmetic and copies ran while one was open for 0% -> 0% of each run, Pallas kernels for 0% -> 0%
where the time goes in v1:
time: 200 us; the launch traced here: 197 us
  Pallas kernels  181 us (90%)
  local copies, waits for them, and re-layouts  13 us (6%)
  other arithmetic  2.2 us (1%)
    pallas_call x1, Pallas kernels, on_device(): pl.pallas_call(functools.partial(kernel, (clients, shards, sub, units, un...  181 us
    unnamed x7, local copies, waits for them, and re-layouts  4.74 us

profile of v1, /device:TPU:0, one launch (start us, length us, event | category | flops | bytes accessed | tf_op | source)
XLA Modules:
  0.0 196.8 jit_solution(11294038705574356204)
XLA Ops:
  0.6 0.0 copy-start
  0.6 1.0 copy-done
  1.7 0.6 dynamic-slice_bitcast_fusion.1.noise_p
  2.3 1.9 reshape.19
  4.2 0.1 slice.9
  4.3 0.0 copy-start.2
  4.3 0.1 copy.11
  4.5 0.7 dynamic-slice_bitcast_fusion.noise_q
  5.1 0.8 copy-done.2
  5.9 2.9 %copy.12.start = bf16[14336,64]{1,0:T(8,128)(2,1)} copy(bf16[14336,64]{0,1:T(8,128)(2,1)S(1)} %copy-done.2) | data formatting | bytes 3670016 | tf_op args[1]
  8.8 180.9 %shard_map.59 = (f32[8,64,128]{2,1,0:T(8,128)}, f32[7,8,32,128]{3,2,1,0:T(8,128)}) custom-call(bf16[1,1024,14336]{2,1,0:T(8,128)(2,1)} %delta_hbm.1, bf16[14336,64]{1,0:T(8,128)(2,1)} %copy.12.start, f32[2,64,128]{2,1,0:T(8,128)} %dynamic-slice_bitcast_fusion.1.noise_p, f32[7,32,128]{2,1,0:T(8,128)} %dynamic-slice_bitcast_fusion.noise_q), custom_call_target="tpu_custom_call" | custom-call | flops 7516192768 | bytes 29360128 | tf_op jit(solution)/shard_map/pallas_call | solution.py:371
  189.8 1.7 copy_bitcast_fusion
  191.4 0.0 copy-start.1
  191.4 1.9 copy.14
  193.3 1.3 reshape.22
  194.6 0.0 copy-done.1
  194.6 2.2 %bitcast_add_fusion = f32[3584,64]{0,1:T(8,128)} fusion(f32[3584,64]{0,1:T(8,128)} %reshape.22, f32[2,3584,64]{1,2,0:T(8,128)S(1)} %copy-done.1), kind=kLoop, calls=%fused_computation | loop fusion | flops 229376 | bytes 2752512 | tf_op jit(solution)/shard_map/add | solution.py:427
Async XLA Ops:
  0.6 1.0 copy-start
  4.3 1.5 copy-start.2
  191.4 3.2 %copy-start.1 = (f32[2,3584,64]{1,2,0:T(8,128)S(1)}, f32[2,3584,64]{1,2,0:T(8,128)}, u32[]{:S(2)}) copy-start(f32[2,3584,64]{1,2,0:T(8,128)} %param.7) | copy-start | bytes 5505028

commit v2 on v1

v2 whole, which is shorter than its diff:
```python
import functools
import math

import jax
import jax.numpy as jnp
from jax import lax
from jax.experimental import pallas as pl
from jax.experimental.pallas import tpu as pltpu
from jax.sharding import PartitionSpec as P

ITERS = 2
EPS = 1e-06
CLIP_FRACTION = 0.5
LANES = 128
MESH = pl.DeviceIdType.MESH
F32 = jnp.float32
BF16 = jnp.bfloat16
HIGH = lax.Precision.HIGHEST


def nt(a, b, precision=None):
    return lax.dot_general(
        a, b, (((1,), (1,)), ((), ())), precision=precision, preferred_element_type=F32
    )


def inverse_lower(gram):
    n = gram.shape[0]
    tall = 8
    rows = lax.broadcasted_iota(jnp.int32, (n, n), 0)
    cols = lax.broadcasted_iota(jnp.int32, (n, n), 1)
    eye = (rows == cols).astype(F32)
    work = jnp.concatenate([gram, eye], axis=1)
    work = [work[i : i + tall] for i in range(0, n, tall)]
    at = lax.broadcasted_iota(jnp.int32, (tall, 2 * n), 0)
    done = []
    for j in range(n):
        b, r = j // tall, j % tall
        row = work[b][r : r + 1]
        done.append(row if r == 0 else jnp.where(at == r, row, done.pop()))
        if r == 0:
            done[-1] = jnp.broadcast_to(row, (tall, 2 * n))
        step = row * (1.0 / row[:, j : j + 1])
        for i in range(b, n // tall):
            work[i] = work[i] - work[i][:, j : j + 1] * step
    done = jnp.concatenate(done, axis=0)
    pivots = jnp.sum(done[:, :n] * eye, axis=1, keepdims=True)
    return done[:, n:] * (1.0 / jnp.sqrt(pivots))


def kernel(
    sizes, delta_hbm, start_hbm, noise_p_hbm, noise_q_hbm, basis_ref, coeffs_ref,
    delta, start, noise_p, noise_q, slabs, acc, sq_buf, sq_all, p_send, p_recv, p_all, g_buf, pb,
    core_send, core_recv, own, y_send, y_recv, z_send, z_recv, q_all, q_last,
    l_own, l_client, l_part, l_shard,
    load_sem, extra_sem, small_send, small_recv, p_sems, g_sems, core_sems, y_sems, z_sems,
    a_sems, ax_sems, ay_sems, ac_sems, f_sems, fx_sems, lc_sems, ls_sems,
):
    clients, shards, minor, sub, units, unit, chunks, groups = sizes
    major = clients // minor
    ys = shards // 2
    rows, full = delta.shape
    rank = start.shape[0]
    piece = rows // clients
    wide = sub * LANES
    span = units * wide
    me_c = lax.axis_index("client")
    me_s = lax.axis_index("shard")
    me_a, me_b = me_c // minor, lax.rem(me_c, minor)
    core = lax.rem(me_s, 2)
    me_y = me_s // 2
    chunk = full // chunks

    def load(i):
        return pltpu.make_async_copy(
            delta_hbm.at[0, :, pl.ds(i * chunk, chunk)],
            delta.at[:, pl.ds(i * chunk, chunk)],
            load_sem.at[i],
        )

    if piece % LANES == 0:
        mine_p = noise_p_hbm.at[:, :, pl.ds(pl.multiple_of(me_c * piece, LANES), piece)]
    else:
        mine_p = noise_p_hbm
    extras = [
        pltpu.make_async_copy(start_hbm, start, extra_sem.at[0]),
        pltpu.make_async_copy(mine_p, noise_p, extra_sem.at[1]),
        pltpu.make_async_copy(noise_q_hbm.at[0], noise_q, extra_sem.at[2]),
    ]
    extras[0].start()
    for i in range(chunks):
        load(i).start()
    extras[1].start()
    extras[2].start()

    barrier = pltpu.get_barrier_semaphore()
    for d in range(1, clients):
        pl.semaphore_signal(
            barrier, inc=1, device_id=(lax.rem(me_c + d, clients), me_s), device_id_type=MESH
        )
    for d in range(1, shards):
        pl.semaphore_signal(
            barrier, inc=1, device_id=(me_c, lax.rem(me_s + d, shards)), device_id_type=MESH
        )

    def send(src, dst, sems, index, device):
        return pltpu.make_async_remote_copy(
            src_ref=src, dst_ref=dst,
            send_sem=sems.at[(0,) + index], recv_sem=sems.at[(1,) + index],
            device_id=device, device_id_type=MESH,
        )

    def to_client(d):
        return (lax.rem(me_c + d, clients), me_s)

    def to_shard(d):
        return (me_c, lax.rem(me_s + d, shards))

    def to_major(d):
        return (lax.rem(me_a + d, major) * minor + me_b, me_s)

    def to_minor(d):
        return (me_a * minor + lax.rem(me_b + d, minor), me_s)

    def came_from(da, db):
        return lax.rem(me_a + major - da, major) * minor + lax.rem(me_b + minor - db, minor)

    to_core = (me_c, 2 * me_y + 1 - core)

    def to_slabs(v):
        v = jnp.concatenate([v[:, t * LANES : (t + 1) * LANES] for t in range(sub)], axis=0)
        return v.reshape(clients, unit, LANES)

    def from_slabs(v):
        v = v.reshape(sub * rank, LANES)
        return jnp.concatenate([v[t * rank : (t + 1) * rank] for t in range(sub)], axis=1)

    extras[0].wait()

    def start_sum(i, total):
        v = start[:, pl.ds(pl.multiple_of(i * wide, LANES), wide)].astype(F32)
        return total + jnp.sum(v * v, axis=0, keepdims=True)

    level0 = jnp.sqrt(
        jnp.sum(lax.fori_loop(0, full // wide, start_sum, jnp.zeros((1, wide), F32)), axis=1, keepdims=True)
        / rank
    )

    acc[...] = jnp.zeros_like(acc)
    step = 512
    total = jnp.zeros((8, step), F32)
    for i in range(chunks):
        load(i).wait()

        def first(j, total, i=i):
            at = pl.multiple_of(i * chunk + j * step, step)
            acc[...] += nt(delta[:, pl.ds(at, step)], start[:, pl.ds(at, step)])

            def squares(r, t):
                v = delta[pl.ds(pl.multiple_of(r * 128, 128), 128), pl.ds(at, step)].astype(F32)
                return t + jnp.sum((v * v).reshape(16, 8, step), axis=0)

            return lax.fori_loop(0, rows // 128, squares, total)

        total = lax.fori_loop(0, chunk // step, first, total)

    pl.semaphore_wait(barrier, clients + shards - 2)

    mine = jnp.sum(jnp.sum(total, axis=0, keepdims=True), axis=1, keepdims=True)
    sq_buf[...] = jnp.broadcast_to(mine, (8, LANES))
    sq_copies = [
        pltpu.make_async_remote_copy(
            src_ref=sq_buf, dst_ref=sq_all.at[d - 1],
            send_sem=small_send.at[d - 1], recv_sem=small_recv.at[d - 1],
            device_id=to_shard(d), device_id_type=MESH,
        )
        for d in range(1, shards)
    ]
    for c in sq_copies:
        c.start()
    extras[1].wait()
    extras[2].wait()
    for k in range(units):
        slabs[k] = to_slabs(noise_q[:, k * wide : (k + 1) * wide])

    for it in range(ITERS):
        for d in range(clients):
            c = lax.rem(me_c + d, clients)
            v = acc[pl.ds(pl.multiple_of(c * piece, piece), piece), :]
            p_send[it, d] = v.T
        if it == 0:
            level = level0
            sumsq = sq_buf[0:1, 0:1]
            for d, c in enumerate(sq_copies, 1):
                c.wait()
                sumsq = sumsq + sq_all[d - 1, 0:1, 0:1]
            count = rows * shards * full
            factor = jnp.minimum(1.0, CLIP_FRACTION * math.sqrt(count) / jnp.sqrt(sumsq + EPS))
        copies = [
            send(p_send.at[it, d], p_recv.at[it, d], p_sems, (it, 0, d), to_client(d))
            for d in range(1, clients)
        ]
        for d, c in enumerate(copies, 1):
            p_send[it, d] = p_send[it, d] * factor
            c.start()
        v = p_send[it, 0] * factor + level * noise_p[it]
        for d, c in enumerate(copies, 1):
            c.wait()
            v = v + p_recv[it, d]
        p_all[it, me_c] = v
        copies = [
            send(p_all.at[it, me_c], p_all.at[it, me_c], p_sems, (it, 1, d), to_client(d))
            for d in range(1, clients)
        ]
        for c in copies:
            c.start()
        for c in copies:
            c.wait()

        panel = jnp.concatenate([p_all[it, c] for c in range(clients)], axis=1)
        gram = nt(panel, panel, HIGH)
        g_buf[it, 0] = gram
        copies = [
            send(g_buf.at[it, 0], g_buf.at[it, d], g_sems, (it, d), to_shard(d))
            for d in range(1, shards)
        ]
        for c in copies:
            c.start()
        for d, c in enumerate(copies, 1):
            c.wait()
            gram = gram + g_buf[it, d]
        panel = jnp.dot(inverse_lower(gram), panel, precision=HIGH, preferred_element_type=F32)
        pb[...] = panel.astype(BF16)
        if it == ITERS - 1:
            basis_ref[...] = panel

        def block(owner, k):
            at = pl.multiple_of(owner * span + k * wide, LANES)
            return to_slabs(factor * jnp.dot(pb[...], delta[:, pl.ds(at, wide)], preferred_element_type=F32))

        y_copies = []
        for dy in list(range(1, ys)) + [0]:
            to_y = lax.rem(me_y + dy, ys)
            core_copies = []
            for g, (k0, k1) in enumerate(groups):

                def other(k, _, to_y=to_y, dy=dy):
                    core_send[it, dy, k] = block(2 * to_y + 1 - core, k)
                    return 0

                lax.fori_loop(k0, k1, other, 0)
                part = pl.ds(k0, k1 - k0)
                c = send(core_send.at[it, dy, part], core_recv.at[it, dy, part], core_sems, (it, dy, g), to_core)
                c.start()
                core_copies.append(c)

            for g, (k0, k1) in enumerate(groups):

                def same(k, _, to_y=to_y):
                    own[k] = block(2 * to_y + core, k)
                    return 0

                def add_core(k, _, dy=dy):
                    v = own[k] + core_recv[it, dy, k]
                    if dy > 0:
                        y_send[it, dy - 1, k] = v.astype(BF16)
                    else:
                        own[k] = v
                    return 0

                lax.fori_loop(k0, k1, same, 0)
                core_copies[g].wait()
                lax.fori_loop(k0, k1, add_core, 0)
                if dy > 0:
                    part = pl.ds(k0, k1 - k0)
                    c = send(
                        y_send.at[it, dy - 1, part], y_recv.at[it, dy - 1, part],
                        y_sems, (it, dy, g), (me_c, 2 * to_y + core),
                    )
                    c.start()
                    y_copies.append((g, c))
        z_copies = []
        for g, (k0, k1) in enumerate(groups):
            for h, c in y_copies:
                if h == g:
                    c.wait()

            def add_y(k, _):
                v = own[k]
                for d in range(1, ys):
                    v = v + y_recv[it, d - 1, k].astype(F32)
                own[k] = v
                for c in range(clients):
                    z_send[it, c, k] = v[c].astype(BF16)
                return 0

            lax.fori_loop(k0, k1, add_y, 0)
            part = pl.ds(k0, k1 - k0)
            for d in range(1, clients):
                c = send(
                    z_send.at[it, lax.rem(me_c + d, clients), part], z_recv.at[it, d, part],
                    z_sems, (it, d, g), to_client(d),
                )
                c.start()
                z_copies.append((g, c))

        square = jnp.zeros((1, LANES), F32)
        for g, (k0, k1) in enumerate(groups):
            for h, c in z_copies:
                if h == g:
                    c.wait()
            for k in range(k0, k1):
                v = own[k, me_c]
                for d in range(1, clients):
                    v = v + z_recv[it, d, k].astype(F32)
                if it < ITERS - 1:
                    v = v + slabs[k, me_c]
                    square = square + jnp.sum(v * v, axis=0, keepdims=True)
                    q_all[me_s, k, me_c] = v.astype(BF16)
                else:
                    q_last[k, me_c] = v

        if it == ITERS - 1:
            here = q_last.at[:, me_c]
            copies = [send(here, here, f_sems, (d,), to_major(d)) for d in range(1, major)]
            for c in copies:
                c.start()
            passed = []
            for da in range(major):
                if da > 0:
                    copies[da - 1].wait_recv()
                here = q_last.at[:, came_from(da, 0)]
                for db in range(1, minor):
                    c = send(here, here, fx_sems, (da, db), to_minor(db))
                    c.start()
                    passed.append((da, db, c))
            for da, db, _ in passed:
                there = q_last.at[:, came_from(da, db)]
                send(there, there, fx_sems, (da, db), to_minor(db)).wait_recv()
            for c in copies + [c for _, _, c in passed]:
                c.wait_send()
            for k in range(units):
                coeffs_ref[:, k * wide : (k + 1) * wide] = from_slabs(q_last[k])
            continue

        part_sum = jnp.sum(square, axis=1, keepdims=True)
        l_own[...] = jnp.broadcast_to(part_sum, (8, LANES))
        here = q_all.at[me_s, :, me_c]
        copies = [send(here, here, a_sems, (d,), to_major(d)) for d in range(1, major)]
        l_copies = [send(l_own, l_client.at[d - 1], lc_sems, (d,), to_client(d)) for d in range(1, clients)]
        for c in copies + l_copies:
            c.start()
        sent = []

        def pass_on(da, db):
            n = da * minor + db
            here = q_all.at[me_s, :, came_from(da, db)]
            for dy in range(1, ys):
                sent.append(send(here, here, ay_sems, (n, dy), (me_c, 2 * lax.rem(me_y + dy, ys) + core)))
                sent[-1].start()
            sent.append(send(here, here, ac_sems, (n, 0), to_core))
            sent[-1].start()

        for da in range(major):
            if da > 0:
                copies[da - 1].wait_recv()
            here = q_all.at[me_s, :, came_from(da, 0)]
            for db in range(1, minor):
                sent.append(send(here, here, ax_sems, (da, db), to_minor(db)))
                sent[-1].start()
            pass_on(da, 0)
        for da in range(major):
            for db in range(1, minor):
                there = q_all.at[me_s, :, came_from(da, db)]
                send(there, there, ax_sems, (da, db), to_minor(db)).wait_recv()
                pass_on(da, db)
        for d, c in enumerate(l_copies, 1):
            c.wait()
            part_sum = part_sum + l_client[d - 1, 0:1, 0:1]
        l_part[...] = jnp.broadcast_to(part_sum, (8, LANES))
        l_copies = [send(l_part, l_shard.at[d - 1], ls_sems, (d,), to_shard(d)) for d in range(1, shards)]
        for c in l_copies:
            c.start()

        def multiply(owner):
            def body(k, _):
                at = pl.multiple_of(owner * span + k * wide, LANES)
                v = from_slabs(q_all[owner, k].astype(F32)).astype(BF16)
                acc[...] += nt(delta[:, pl.ds(at, wide)], v)
                return 0

            lax.fori_loop(0, units, body, 0)

        order = [(da, db) for db in range(minor) for da in range(major)]
        acc[...] = jnp.zeros_like(acc)
        multiply(me_s)
        for dy in range(1, ys):
            owner = 2 * lax.rem(me_y + ys - dy, ys) + core
            for da, db in order:
                n = da * minor + db
                there = q_all.at[owner, :, came_from(da, db)]
                send(there, there, ay_sems, (n, dy), to_core).wait_recv()
                sent.append(send(there, there, ac_sems, (n, dy), to_core))
                sent[-1].start()
        for dy in range(ys):
            owner = 2 * lax.rem(me_y + ys - dy, ys) + 1 - core
            for da, db in order:
                there = q_all.at[owner, :, came_from(da, db)]
                send(there, there, ac_sems, (da * minor + db, dy), to_core).wait_recv()
            multiply(owner)
            if dy > 0:
                continue
            for d in range(1, ys):
                multiply(2 * lax.rem(me_y + ys - d, ys) + core)
        for c in sent + copies:
            c.wait_send()
        for d, c in enumerate(l_copies, 1):
            c.wait()
            part_sum = part_sum + l_shard[d - 1, 0:1, 0:1]
        level = jnp.sqrt(part_sum / rank)


def on_device(clients, shards, delta, start_coeffs, noise_p, noise_q):
    rows, full = delta.shape[1:]
    rank = start_coeffs.shape[1]
    ys = shards // 2
    minor = 2
    major = clients // minor
    piece = rows // clients
    tiles = full // shards // LANES
    sub = next(
        s for s in range(1, tiles + 1)
        if tiles % s == 0 and (s * rank) % (8 * clients) == 0 and s * rank >= 32 * clients
    )
    units = tiles // sub
    unit = sub * rank // clients
    chunks = 7
    bounds = sorted({round(units * i / 3) for i in range(4)})
    groups = list(zip(bounds[:-1], bounds[1:]))
    parts = len(groups)
    panel_noise = noise_p.transpose(0, 2, 1)
    if piece % LANES:
        me = lax.axis_index("client")
        panel_noise = lax.dynamic_slice_in_dim(panel_noise, me * piece, piece, axis=2)

    dma = pltpu.SemaphoreType.DMA
    slab = (units, clients, unit, LANES)
    basis, coeffs = pl.pallas_call(
        functools.partial(kernel, (clients, shards, minor, sub, units, unit, chunks, groups)),
        out_shape=(
            jax.ShapeDtypeStruct((rank, rows), F32),
            jax.ShapeDtypeStruct((rank, full // shards), F32),
        ),
        in_specs=[pl.BlockSpec(memory_space=pl.ANY)] * 4,
        out_specs=[pl.BlockSpec(memory_space=pltpu.VMEM)] * 2,
        scratch_shapes=[
            pltpu.VMEM((rows, full), BF16),
            pltpu.VMEM((rank, full), BF16),
            pltpu.VMEM((ITERS, rank, piece), F32),
            pltpu.VMEM((rank, full // shards), F32),
            pltpu.VMEM(slab, F32),
            pltpu.VMEM((rows, rank), F32),
            pltpu.VMEM((8, LANES), F32),
            pltpu.VMEM((shards - 1, 8, LANES), F32),
            pltpu.VMEM((ITERS, clients, rank, piece), F32),
            pltpu.VMEM((ITERS, clients, rank, piece), F32),
            pltpu.VMEM((ITERS, clients, rank, piece), F32),
            pltpu.VMEM((ITERS, shards, rank, rank), F32),
            pltpu.VMEM((rank, rows), BF16),
            pltpu.VMEM((ITERS, ys) + slab, F32),
            pltpu.VMEM((ITERS, ys) + slab, F32),
            pltpu.VMEM(slab, F32),
            pltpu.VMEM((ITERS, ys - 1) + slab, BF16),
            pltpu.VMEM((ITERS, ys - 1) + slab, BF16),
            pltpu.VMEM((ITERS, clients, units, unit, LANES), BF16),
            pltpu.VMEM((ITERS, clients, units, unit, LANES), BF16),
            pltpu.VMEM((shards,) + slab, BF16),
            pltpu.VMEM(slab, F32),
            pltpu.VMEM((8, LANES), F32),
            pltpu.VMEM((clients - 1, 8, LANES), F32),
            pltpu.VMEM((8, LANES), F32),
            pltpu.VMEM((shards - 1, 8, LANES), F32),
            dma((chunks,)),
            dma((3,)),
            dma((shards - 1,)),
            dma((shards - 1,)),
            dma((2, ITERS, 2, clients)),
            dma((2, ITERS, shards)),
            dma((2, ITERS, ys, parts)),
            dma((2, ITERS, ys, parts)),
            dma((2, ITERS, clients, parts)),
            dma((2, major)),
            dma((2, major, minor)),
            dma((2, clients, ys)),
            dma((2, clients, ys)),
            dma((2, major)),
            dma((2, major, minor)),
            dma((2, clients)),
            dma((2, shards)),
        ],
        compiler_params=pltpu.CompilerParams(
            collective_id=0, has_side_effects=True, vmem_limit_bytes=60 * 1024 * 1024
        ),
        cost_estimate=pl.CostEstimate(
            flops=8 * rows * full * rank, bytes_accessed=2 * rows * full, transcendentals=0
        ),
    )(delta, start_coeffs.T, panel_noise, noise_q.transpose(0, 2, 1))
    return math.sqrt(rows * shards) * basis.T, coeffs.T + noise_q[ITERS - 1]


def solution(mesh):
    placed = (P("client", "shard", None), P(), P(None, "shard", None), P(None, "shard", None))
    return jax.shard_map(
        functools.partial(on_device, mesh.shape["client"], mesh.shape["shard"]),
        mesh=mesh,
        in_specs=placed,
        out_specs=(P("shard", None), P("shard", None)),
        check_vma=False,
    )
```

time: 200 us -> 163 us (0.81); the launches traced: 197 us -> 162 us
  Pallas kernels: 181 us -> 158 us
  local copies, waits for them, and re-layouts: 13 us -> 0.01 us
    pallas_call x1, Pallas kernels: 181 us -> 158 us  [on_device(): pl.pallas_call(functools.partial(kernel, (clients, shards, minor, sub, un...]
    reshape x3 -> x0, local copies, waits for them, and re-layouts: 4.89 us -> none  [the longest x1 1.93 us: on_device(): noise_q.reshape(ITERS, units, sub, LANES, rank).transpose(0, 1, 2, 4, 3)]
    unnamed x7 -> x2, local copies, waits for them, and re-layouts: 4.74 us -> 0.01 us
    transpose x2 -> x0, local copies, waits for them, and re-layouts: 2.54 us -> none  [the longest x1 1.9 us: on_device(): coeffs.reshape(units, sub, rank, LANES).transpose(0, 1, 3, 2)]
where the time goes in v2:
time: 163 us; the launch traced here: 162 us
  Pallas kernels  158 us (97%)
  other arithmetic  3.87 us (2%)
    pallas_call x1, Pallas kernels, on_device(): pl.pallas_call(functools.partial(kernel, (clients, shards, minor, sub, un...  158 us

profile of v2, /device:TPU:0, one launch (start us, length us, event | category | flops | bytes accessed | tf_op | source)
XLA Modules:
  0.0 162.3 jit_solution(17660998597506631005)
XLA Ops:
  0.6 0.0 copy-start
  0.6 157.8 %shard_map.59 = (f32[64,1024]{1,0:T(8,128)}, f32[64,3584]{1,0:T(8,128)}) custom-call(bf16[1,1024,14336]{2,1,0:T(8,128)(2,1)} %delta_hbm.1, bf16[64,14336]{1,0:T(8,128)(2,1)} %bitcast.10, f32[2,64,1024]{2,1,0:T(8,128)} %bitcast.11, f32[2,64,3584]{2,1,0:T(8,128)} %bitcast.9), custom_call_target="tpu_custom_call" | custom-call | flops 7516192768 | bytes 29360128 | tf_op jit(solution)/shard_map/pallas_call | solution.py:448
  158.4 1.7 %multiply_bitcast_fusion = f32[1024,64]{0,1:T(8,128)} fusion(f32[64,1024]{1,0:T(8,128)} %get-tuple-element.4), kind=kLoop, calls=%fused_computation.1 | loop fusion | flops 65536 | bytes 524288 | tf_op jit(solution)/shard_map/mul | solution.py:508
  160.1 0.0 copy-done
  160.1 2.2 %bitcast_add_fusion = f32[3584,64]{0,1:T(8,128)} fusion(f32[64,3584]{1,0:T(8,128)} %get-tuple-element.5, f32[2,3584,64]{1,2,0:T(8,128)S(1)} %copy-done), kind=kLoop, calls=%fused_computation | loop fusion | flops 229376 | bytes 2752512 | tf_op jit(solution)/shard_map/add | solution.py:508
Async XLA Ops:
  0.6 159.5 %copy-start = (f32[2,3584,64]{1,2,0:T(8,128)S(1)}, f32[2,3584,64]{1,2,0:T(8,128)}, u32[]{:S(2)}) copy-start(f32[2,3584,64]{1,2,0:T(8,128)} %param.7) | copy-start | bytes 5505028

commit v3 on v2

--- a/solution.py
+++ b/solution.py
@@ -33,16 +33,37 @@
     work = jnp.concatenate([gram, eye], axis=1)
     work = [work[i : i + tall] for i in range(0, n, tall)]
     at = lax.broadcasted_iota(jnp.int32, (tall, 2 * n), 0)
+    many = 4
     done = []
-    for j in range(n):
+    for j in range(0, n, many):
         b, r = j // tall, j % tall
-        row = work[b][r : r + 1]
-        done.append(row if r == 0 else jnp.where(at == r, row, done.pop()))
+        top = work[b]
+        rows4 = [top[r + p : r + p + 1] for p in range(many)]
+        head = [
+            [jnp.broadcast_to(rows4[p][:, j + q : j + q + 1], (1, 2 * n)) if q >= p else None for q in range(many)]
+            for p in range(many)
+        ]
+        inv = []
+        for p in range(many):
+            inv.append(1.0 / head[p][p])
+            for q in range(p + 1, many):
+                times = head[p][q] * inv[p]
+                rows4[q] = rows4[q] - times * rows4[p]
+                for t in range(q, many):
+                    head[q][t] = head[q][t] - times * head[p][t]
         if r == 0:
-            done[-1] = jnp.broadcast_to(row, (tall, 2 * n))
-        step = row * (1.0 / row[:, j : j + 1])
-        for i in range(b, n // tall):
-            work[i] = work[i] - work[i][:, j : j + 1] * step
+            done.append(jnp.zeros((tall, 2 * n), F32))
+        for p in range(many):
+            done[-1] = jnp.where(at == r + p, rows4[p], done[-1])
+        for i in range(b if r + many < tall else b + 1, n // tall):
+            old = work[i]
+            col = [jnp.broadcast_to(old[:, j + q : j + q + 1], (tall, 2 * n)) for q in range(many)]
+            for p in range(many):
+                times = col[p] * inv[p]
+                old = old - times * rows4[p]
+                for q in range(p + 1, many):
+                    col[q] = col[q] - times * head[p][q]
+            work[i] = old
     done = jnp.concatenate(done, axis=0)
     pivots = jnp.sum(done[:, :n] * eye, axis=1, keepdims=True)
     return done[:, n:] * (1.0 / jnp.sqrt(pivots))
@@ -50,10 +71,10 @@
 
 def kernel(
     sizes, delta_hbm, start_hbm, noise_p_hbm, noise_q_hbm, basis_ref, coeffs_ref,
-    delta, start, noise_p, noise_q, slabs, acc, sq_buf, sq_all, p_send, p_recv, p_all, g_buf, pb,
+    delta, start, noise_p, noise_q, slabs, acc, sq_buf, sq_all, p_turned, p_send, p_recv, p_all, g_buf, pb,
     core_send, core_recv, own, y_send, y_recv, z_send, z_recv, q_all, q_last,
     l_own, l_client, l_part, l_shard,
-    load_sem, extra_sem, small_send, small_recv, p_sems, g_sems, core_sems, y_sems, z_sems,
+    load_sem, extra_sem, small_send, small_recv, p_sems, pa_sems, px_sems, g_sems, core_sems, y_sems, z_sems,
     a_sems, ax_sems, ay_sems, ac_sems, f_sems, fx_sems, lc_sems, ls_sems,
 ):
     clients, shards, minor, sub, units, unit, chunks, groups = sizes
@@ -135,6 +156,29 @@
         v = v.reshape(sub * rank, LANES)
         return jnp.concatenate([v[t * rank : (t + 1) * rank] for t in range(sub)], axis=1)
 
+    def begin(here, sems, key):
+        copies = [send(here, here, sems, key + (d,), to_major(d)) for d in range(1, major)]
+        for c in copies:
+            c.start()
+        return copies
+
+    def finish(first, at, key, sems):
+        passed = []
+        for da in range(major):
+            for g, copies in enumerate(first):
+                if da > 0:
+                    copies[da - 1].wait_recv()
+                here = at(g, came_from(da, 0))
+                for db in range(1, minor):
+                    c = send(here, here, sems, key(g) + (da, db), to_minor(db))
+                    c.start()
+                    passed.append((g, da, db, c))
+        for g, da, db, _ in passed:
+            there = at(g, came_from(da, db))
+            send(there, there, sems, key(g) + (da, db), to_minor(db)).wait_recv()
+        for c in [c for copies in first for c in copies] + [p[3] for p in passed]:
+            c.wait_send()
+
     extras[0].wait()
 
     def start_sum(i, total):
@@ -156,11 +200,10 @@
             at = pl.multiple_of(i * chunk + j * step, step)
             acc[...] += nt(delta[:, pl.ds(at, step)], start[:, pl.ds(at, step)])
 
-            def squares(r, t):
-                v = delta[pl.ds(pl.multiple_of(r * 128, 128), 128), pl.ds(at, step)].astype(F32)
-                return t + jnp.sum((v * v).reshape(16, 8, step), axis=0)
-
-            return lax.fori_loop(0, rows // 128, squares, total)
+            for r in range(0, rows, 128):
+                v = delta[r : r + 128, pl.ds(at, step)].astype(F32)
+                total = total + jnp.sum((v * v).reshape(16, 8, step), axis=0)
+            return total
 
         total = lax.fori_loop(0, chunk // step, first, total)
 
@@ -187,7 +230,7 @@
         for d in range(clients):
             c = lax.rem(me_c + d, clients)
             v = acc[pl.ds(pl.multiple_of(c * piece, piece), piece), :]
-            p_send[it, d] = v.T
+            p_turned[d] = v.T
         if it == 0:
             level = level0
             sumsq = sq_buf[0:1, 0:1]
@@ -197,25 +240,19 @@
             count = rows * shards * full
             factor = jnp.minimum(1.0, CLIP_FRACTION * math.sqrt(count) / jnp.sqrt(sumsq + EPS))
         copies = [
-            send(p_send.at[it, d], p_recv.at[it, d], p_sems, (it, 0, d), to_client(d))
+            send(p_send.at[it, d], p_recv.at[it, d], p_sems, (it, d), to_client(d))
             for d in range(1, clients)
         ]
         for d, c in enumerate(copies, 1):
-            p_send[it, d] = p_send[it, d] * factor
+            p_send[it, d] = (p_turned[d] * factor).astype(BF16)
             c.start()
-        v = p_send[it, 0] * factor + level * noise_p[it]
+        v = p_turned[0] * factor + level * noise_p[it]
         for d, c in enumerate(copies, 1):
             c.wait()
-            v = v + p_recv[it, d]
+            v = v + p_recv[it, d].astype(F32)
         p_all[it, me_c] = v
-        copies = [
-            send(p_all.at[it, me_c], p_all.at[it, me_c], p_sems, (it, 1, d), to_client(d))
-            for d in range(1, clients)
-        ]
-        for c in copies:
-            c.start()
-        for c in copies:
-            c.wait()
+        copies = begin(p_all.at[it, me_c], pa_sems, (it,))
+        finish([copies], lambda g, who, it=it: p_all.at[it, who], lambda g, it=it: (it,), px_sems)
 
         panel = jnp.concatenate([p_all[it, c] for c in range(clients)], axis=1)
         gram = nt(panel, panel, HIGH)
@@ -242,9 +279,11 @@
         for dy in list(range(1, ys)) + [0]:
             to_y = lax.rem(me_y + dy, ys)
             core_copies = []
-            for g, (k0, k1) in enumerate(groups):
-
-                def other(k, _, to_y=to_y, dy=dy):
+
+            def run_other(g, to_y=to_y, dy=dy):
+                k0, k1 = groups[g]
+
+                def other(k, _):
                     core_send[it, dy, k] = block(2 * to_y + 1 - core, k)
                     return 0
 
@@ -254,13 +293,14 @@
                 c.start()
                 core_copies.append(c)
 
-            for g, (k0, k1) in enumerate(groups):
-
-                def same(k, _, to_y=to_y):
+            def run_same(g, to_y=to_y, dy=dy):
+                k0, k1 = groups[g]
+
+                def same(k, _):
                     own[k] = block(2 * to_y + core, k)
                     return 0
 
-                def add_core(k, _, dy=dy):
+                def add_core(k, _):
                     v = own[k] + core_recv[it, dy, k]
                     if dy > 0:
                         y_send[it, dy - 1, k] = v.astype(BF16)
@@ -279,6 +319,12 @@
                     )
                     c.start()
                     y_copies.append((g, c))
+
+            run_other(0)
+            for g in range(len(groups)):
+                if g + 1 < len(groups):
+                    run_other(g + 1)
+                run_same(g)
         z_copies = []
         for g, (k0, k1) in enumerate(groups):
             for h, c in y_copies:
@@ -305,6 +351,7 @@
                 z_copies.append((g, c))
 
         square = jnp.zeros((1, LANES), F32)
+        last = []
         for g, (k0, k1) in enumerate(groups):
             for h, c in z_copies:
                 if h == g:
@@ -319,26 +366,16 @@
                     q_all[me_s, k, me_c] = v.astype(BF16)
                 else:
                     q_last[k, me_c] = v
+            if it == ITERS - 1:
+                last.append(begin(q_last.at[pl.ds(k0, k1 - k0), me_c], f_sems, (g,)))
 
         if it == ITERS - 1:
-            here = q_last.at[:, me_c]
-            copies = [send(here, here, f_sems, (d,), to_major(d)) for d in range(1, major)]
-            for c in copies:
-                c.start()
-            passed = []
-            for da in range(major):
-                if da > 0:
-                    copies[da - 1].wait_recv()
-                here = q_last.at[:, came_from(da, 0)]
-                for db in range(1, minor):
-                    c = send(here, here, fx_sems, (da, db), to_minor(db))
-                    c.start()
-                    passed.append((da, db, c))
-            for da, db, _ in passed:
-                there = q_last.at[:, came_from(da, db)]
-                send(there, there, fx_sems, (da, db), to_minor(db)).wait_recv()
-            for c in copies + [c for _, _, c in passed]:
-                c.wait_send()
+            finish(
+                last,
+                lambda g, who: q_last.at[pl.ds(groups[g][0], groups[g][1] - groups[g][0]), who],
+                lambda g: (g,),
+                fx_sems,
+            )
             for k in range(units):
                 coeffs_ref[:, k * wide : (k + 1) * wide] = from_slabs(q_last[k])
             continue
@@ -462,8 +499,9 @@
             pltpu.VMEM((rows, rank), F32),
             pltpu.VMEM((8, LANES), F32),
             pltpu.VMEM((shards - 1, 8, LANES), F32),
-            pltpu.VMEM((ITERS, clients, rank, piece), F32),
-            pltpu.VMEM((ITERS, clients, rank, piece), F32),
+            pltpu.VMEM((clients, rank, piece), F32),
+            pltpu.VMEM((ITERS, clients, rank, piece), BF16),
+            pltpu.VMEM((ITERS, clients, rank, piece), BF16),
             pltpu.VMEM((ITERS, clients, rank, piece), F32),
             pltpu.VMEM((ITERS, shards, rank, rank), F32),
             pltpu.VMEM((rank, rows), BF16),
@@ -484,7 +522,9 @@
             dma((3,)),
             dma((shards - 1,)),
             dma((shards - 1,)),
-            dma((2, ITERS, 2, clients)),
+            dma((2, ITERS, clients)),
+            dma((2, ITERS, major)),
+            dma((2, ITERS, major, minor)),
             dma((2, ITERS, shards)),
             dma((2, ITERS, ys, parts)),
             dma((2, ITERS, ys, parts)),
@@ -493,8 +533,8 @@
             dma((2, major, minor)),
             dma((2, clients, ys)),
             dma((2, clients, ys)),
-            dma((2, major)),
-            dma((2, major, minor)),
+            dma((2, parts, major)),
+            dma((2, parts, major, minor)),
             dma((2, clients)),
             dma((2, shards)),
         ],

time: 163 us -> 151 us (0.926)
  Pallas kernels: 158 us -> 147 us
    pallas_call x1, Pallas kernels: 158 us -> 147 us  [on_device(): pl.pallas_call(functools.partial(kernel, (clients, shards, minor, sub, un...]
where the time goes in v3:
time: 151 us
  Pallas kernels  147 us (97%)
  other arithmetic  3.87 us (3%)
    pallas_call x1, Pallas kernels, on_device(): pl.pallas_call(functools.partial(kernel, (clients, shards, minor, sub, un...  147 us

profile of v3, /device:TPU:0, one launch (start us, length us, event | category | flops | bytes accessed | tf_op | source)
XLA Modules:
  0.0 151.1 jit_solution(14450192572548255202)
XLA Ops:
  0.6 0.0 copy-start
  0.6 146.6 %shard_map.59 = (f32[64,1024]{1,0:T(8,128)}, f32[64,3584]{1,0:T(8,128)}) custom-call(bf16[1,1024,14336]{2,1,0:T(8,128)(2,1)} %delta_hbm.1, bf16[64,14336]{1,0:T(8,128)(2,1)} %bitcast.10, f32[2,64,1024]{2,1,0:T(8,128)} %bitcast.11, f32[2,64,3584]{2,1,0:T(8,128)} %bitcast.9), custom_call_target="tpu_custom_call" | custom-call | flops 7516192768 | bytes 29360128 | tf_op jit(solution)/shard_map/pallas_call | solution.py:485
  147.3 1.7 %multiply_bitcast_fusion = f32[1024,64]{0,1:T(8,128)} fusion(f32[64,1024]{1,0:T(8,128)} %get-tuple-element.4), kind=kLoop, calls=%fused_computation.1 | loop fusion | flops 65536 | bytes 524288 | tf_op jit(solution)/shard_map/mul | solution.py:548
  148.9 0.0 copy-done
  149.0 2.2 %bitcast_add_fusion = f32[3584,64]{0,1:T(8,128)} fusion(f32[64,3584]{1,0:T(8,128)} %get-tuple-element.5, f32[2,3584,64]{1,2,0:T(8,128)S(1)} %copy-done), kind=kLoop, calls=%fused_computation | loop fusion | flops 229376 | bytes 2752512 | tf_op jit(solution)/shard_map/add | solution.py:548
Async XLA Ops:
  0.6 148.3 %copy-start = (f32[2,3584,64]{1,2,0:T(8,128)S(1)}, f32[2,3584,64]{1,2,0:T(8,128)}, u32[]{:S(2)}) copy-start(f32[2,3584,64]{1,2,0:T(8,128)} %param.7) | copy-start | bytes 5505028

commit v4 on v3

--- a/solution.py
+++ b/solution.py
@@ -71,7 +71,7 @@
 
 def kernel(
     sizes, delta_hbm, start_hbm, noise_p_hbm, noise_q_hbm, basis_ref, coeffs_ref,
-    delta, start, noise_p, noise_q, slabs, acc, sq_buf, sq_all, p_turned, p_send, p_recv, p_all, g_buf, pb,
+    delta, start, noise_p, noise_q, slabs, acc, sq_buf, sq_all, p_turned, p_send, p_recv, p_send_last, p_recv_last, p_all, g_buf, pb,
     core_send, core_recv, own, y_send, y_recv, z_send, z_recv, q_all, q_last,
     l_own, l_client, l_part, l_shard,
     load_sem, extra_sem, small_send, small_recv, p_sems, pa_sems, px_sems, g_sems, core_sems, y_sems, z_sems,
@@ -227,6 +227,7 @@
         slabs[k] = to_slabs(noise_q[:, k * wide : (k + 1) * wide])
 
     for it in range(ITERS):
+        p_out, p_in = (p_send_last, p_recv_last) if it == ITERS - 1 else (p_send.at[it], p_recv.at[it])
         for d in range(clients):
             c = lax.rem(me_c + d, clients)
             v = acc[pl.ds(pl.multiple_of(c * piece, piece), piece), :]
@@ -240,16 +241,16 @@
             count = rows * shards * full
             factor = jnp.minimum(1.0, CLIP_FRACTION * math.sqrt(count) / jnp.sqrt(sumsq + EPS))
         copies = [
-            send(p_send.at[it, d], p_recv.at[it, d], p_sems, (it, d), to_client(d))
+            send(p_out.at[d], p_in.at[d], p_sems, (it, d), to_client(d))
             for d in range(1, clients)
         ]
         for d, c in enumerate(copies, 1):
-            p_send[it, d] = (p_turned[d] * factor).astype(BF16)
+            p_out[d] = (p_turned[d] * factor).astype(p_out.dtype)
             c.start()
         v = p_turned[0] * factor + level * noise_p[it]
         for d, c in enumerate(copies, 1):
             c.wait()
-            v = v + p_recv[it, d].astype(F32)
+            v = v + p_in[d].astype(F32)
         p_all[it, me_c] = v
         copies = begin(p_all.at[it, me_c], pa_sems, (it,))
         finish([copies], lambda g, who, it=it: p_all.at[it, who], lambda g, it=it: (it,), px_sems)
@@ -500,8 +501,10 @@
             pltpu.VMEM((8, LANES), F32),
             pltpu.VMEM((shards - 1, 8, LANES), F32),
             pltpu.VMEM((clients, rank, piece), F32),
-            pltpu.VMEM((ITERS, clients, rank, piece), BF16),
-            pltpu.VMEM((ITERS, clients, rank, piece), BF16),
+            pltpu.VMEM((ITERS - 1, clients, rank, piece), BF16),
+            pltpu.VMEM((ITERS - 1, clients, rank, piece), BF16),
+            pltpu.VMEM((clients, rank, piece), F32),
+            pltpu.VMEM((clients, rank, piece), F32),
             pltpu.VMEM((ITERS, clients, rank, piece), F32),
             pltpu.VMEM((ITERS, shards, rank, rank), F32),
             pltpu.VMEM((rank, rows), BF16),

time: 151 us -> 152 us (level)
  no operation moved by 1% of the time
where the time goes in v4:
time: 152 us
  Pallas kernels  147 us (97%)
  other arithmetic  3.87 us (3%)
    pallas_call x1, Pallas kernels, on_device(): pl.pallas_call(functools.partial(kernel, (clients, shards, minor, sub, un...  147 us

profile of v4, /device:TPU:0, one launch (start us, length us, event | category | flops | bytes accessed | tf_op | source)
XLA Modules:
  0.0 152.0 jit_solution(12318348663603883533)
XLA Ops:
  0.6 0.0 copy-start
  0.6 147.5 %shard_map.59 = (f32[64,1024]{1,0:T(8,128)}, f32[64,3584]{1,0:T(8,128)}) custom-call(bf16[1,1024,14336]{2,1,0:T(8,128)(2,1)} %delta_hbm.1, bf16[64,14336]{1,0:T(8,128)(2,1)} %bitcast.10, f32[2,64,1024]{2,1,0:T(8,128)} %bitcast.11, f32[2,64,3584]{2,1,0:T(8,128)} %bitcast.9), custom_call_target="tpu_custom_call" | custom-call | flops 7516192768 | bytes 29360128 | tf_op jit(solution)/shard_map/pallas_call | solution.py:486
  148.1 1.7 %multiply_bitcast_fusion = f32[1024,64]{0,1:T(8,128)} fusion(f32[64,1024]{1,0:T(8,128)} %get-tuple-element.4), kind=kLoop, calls=%fused_computation.1 | loop fusion | flops 65536 | bytes 524288 | tf_op jit(solution)/shard_map/mul | solution.py:551
  149.8 0.0 copy-done
  149.8 2.2 %bitcast_add_fusion = f32[3584,64]{0,1:T(8,128)} fusion(f32[64,3584]{1,0:T(8,128)} %get-tuple-element.5, f32[2,3584,64]{1,2,0:T(8,128)S(1)} %copy-done), kind=kLoop, calls=%fused_computation | loop fusion | flops 229376 | bytes 2752512 | tf_op jit(solution)/shard_map/add | solution.py:551
Async XLA Ops:
  0.6 149.2 %copy-start = (f32[2,3584,64]{1,2,0:T(8,128)S(1)}, f32[2,3584,64]{1,2,0:T(8,128)}, u32[]{:S(2)}) copy-start(f32[2,3584,64]{1,2,0:T(8,128)} %param.7) | copy-start | bytes 5505028
